TPU v7x, 512 devices: a whole 4x4x16 slice. The times are simulated.
512 devices in a mesh: island: 32 (over z_hi, y, core), tensor: 16 (over z_lo, x).
Axes of the slice: x: 4, y: 4, z: 16 (z_hi: 4, z_lo: 4; z = z_hi * 4 + z_lo), core: 2. Of those that a mesh axis runs over, the one named last changes fastest.
Arguments:
- grad_slab: bfloat16 [32, 28672, 384], P('island', 'tensor'), may hold values from -3 to 3
- projector: bfloat16 [28672, 512], P('tensor'), may hold values from -0.25 to 0.25
- first_moment: float32 [32, 512, 384], P('island', 'tensor'), may hold values from -3 to 3
- second_moment: float32 [32, 512, 384], P('island', 'tensor'), may hold values from 0.1 to 1
- momentum: float32 [512, 384], P('tensor'), may hold values from -0.9 to 0.9
Outputs:
- update: bfloat16 [28672, 384], P('tensor')
- velocity: float32 [512, 384], P('tensor')
All inputs are finite; a program needn't handle non-finite values.
Results may differ from a plain program's by a relative error of at most 0.0049.
Values may be sent and summed in bfloat16 or wider, within the bound.
A program may use at most 64 MiB of HBM per device.

v0:
```python
import jax
import jax.numpy as jnp
from jax import lax
from jax.sharding import PartitionSpec as P

BETA_ONE = 0.9
BETA_TWO = 0.95
EPSILON = 1e-08
NESTEROV = 0.9
OUTER_RATE = 0.7


def local(grad_slab, projector, first_moment, second_moment, momentum):
    rows_here = first_moment.shape[1]
    gradient = grad_slab[0]
    partial_sum = lax.dot_general(
        projector, gradient, (((0,), (0,)), ((), ())), preferred_element_type=jnp.float32
    )
    summed = lax.psum(partial_sum, "tensor")
    offset = lax.axis_index("tensor") * rows_here
    projected = lax.dynamic_slice_in_dim(summed, offset, rows_here, 0)
    first = BETA_ONE * first_moment[0] + (1.0 - BETA_ONE) * projected
    second = BETA_TWO * second_moment[0] + (1.0 - BETA_TWO) * projected * projected
    pseudo = first / (jnp.sqrt(second) + EPSILON)
    averaged = lax.psum(pseudo, "island") / lax.axis_size("island")
    velocity = NESTEROV * momentum + averaged
    outer_step = (averaged + NESTEROV * velocity).astype(jnp.bfloat16)
    back_projected = jnp.dot(
        projector,
        lax.all_gather(outer_step, "tensor", axis=0, tiled=True),
        preferred_element_type=jnp.float32,
    )
    update = (OUTER_RATE * back_projected).astype(jnp.bfloat16)
    return (update, velocity)


def solution(mesh):
    in_specs = (
        P("island", "tensor", None),
        P("tensor", None),
        P("island", "tensor", None),
        P("island", "tensor", None),
        P("tensor", None),
    )
    out_specs = (P("tensor", None), P("tensor", None))
    return jax.shard_map(local, mesh=mesh, in_specs=in_specs, out_specs=out_specs, check_vma=False)
```

profile of v0, /device:TPU:128, one launch (start us, length us, event | category | flops | bytes accessed | tf_op | source)
XLA Modules:
  0.0 409.8 jit_solution(6052851825746047595)
XLA Ops:
  7.2 0.0 copy-start
  7.2 0.0 copy-start.1
  7.2 0.0 copy-start.2
  7.2 0.0 copy-start.3
  7.2 0.0 all-reduce.2.cloned.1.call-start
  7.3 1.4 copy-done
  8.7 3.4 fusion.2
  12.0 0.0 all-reduce.2.cloned.1.call-update
  12.1 175.9 %all-reduce.2.cloned.1.call-done = f32[512,384]{1,0:T(8,128)} async-done(((f32[512,384]{1,0:T(8,128)}), f32[512,384]{1,0:T(8,128)}) %all-reduce.2.cloned.1.call-update) | async-done | bytes 786448 | tf_op jit(solution)/shard_map/psum | solution.py:19
  188.0 0.0 copy-done.1
  188.0 0.0 copy-done.2
  188.0 0.8 fusion.7
  188.8 166.9 %psum.15 = f32[32,384]{1,0:T(8,128)S(1)} all-reduce(f32[32,384]{1,0:T(8,128)S(1)} %fusion.7), channel_id=1, replica_groups=mesh['island'=32,'tensor'=16] {'island'}, use_global_device_ids=true, to_apply=%region_1.0 | all-reduce | flops 12288 | bytes 98304 | tf_op jit(solution)/shard_map/psum | solution.py:25
  355.8 0.0 copy-done.3
  355.8 0.6 add_convert_fusion
  356.4 44.1 %all_gather.3 = bf16[512,384]{1,0:T(8,128)(2,1)S(1)} all-gather(bf16[32,384]{1,0:T(8,128)(2,1)S(1)} %get-tuple-element.4), channel_id=1, replica_groups=mesh['island'=32,'tensor'=16] {'tensor'}, dimensions={0}, use_global_device_ids=true | all-gather | bytes 417792 | tf_op jit(solution)/shard_map/all_gather | solution.py:30
  400.5 0.9 fusion.1
  401.5 1.5 copy.7
Async XLA Ops:
  7.2 1.5 copy-start
  7.2 180.8 %copy-start.1 = (f32[1,32,384]{2,1,0:T(8,128)S(1)}, f32[1,32,384]{2,1,0:T(8,128)}, u32[]{:S(2)}) copy-start(f32[1,32,384]{2,1,0:T(8,128)} %param.8) | copy-start | bytes 147460
  7.2 180.8 %copy-start.2 = (f32[1,32,384]{2,1,0:T(8,128)S(1)}, f32[1,32,384]{2,1,0:T(8,128)}, u32[]{:S(2)}) copy-start(f32[1,32,384]{2,1,0:T(8,128)} %param.7) | copy-start | bytes 147460
  7.2 348.6 %copy-start.3 = (f32[32,384]{1,0:T(8,128)S(1)}, f32[32,384]{1,0:T(8,128)}, u32[]{:S(2)}) copy-start(f32[32,384]{1,0:T(8,128)} %param.9) | copy-start | bytes 147460
  7.2 180.8 %all-reduce.2.cloned.1.call-start = ((), (), s32[]{:S(2)}) async-start(), calls=%async_computation | async-start | bytes 1572864 | tf_op jit(solution)/shard_map/psum | solution.py:19
Sparse Core Ops, SparseCore 0:
  12.2 175.7 all-reduce.1
where the time goes:
time: 410 us
  blocking collectives  211 us (51%)
  waiting for transfers between devices  176 us (43%)
  between operations  14.1 us (3%)
  matrix products  4.29 us (1%)
    psum x1, waiting for transfers between devices, local(): summed = lax.psum(partial_sum, 'tensor')  176 us
    psum x1, blocking collectives, local(): averaged = lax.psum(pseudo, 'island') / lax.axis_size('island')  167 us
    all_gather x1, blocking collectives, local(): lax.all_gather(outer_step, 'tensor', axis=0, tiled=True)  44.1 us
  transfers between devices with their start and end apart: 1, of which 1 were waited for; matrix products, arithmetic and copies ran while one was open for 0% of the time, Pallas kernels for 0%

commit v1 on v0

v1 whole, which is shorter than its diff:
```python
import functools

import jax
import jax.numpy as jnp
from jax import lax
from jax.experimental import pallas as pl
from jax.experimental.pallas import tpu as pltpu
from jax.sharding import PartitionSpec as P

BETA_ONE = 0.9
BETA_TWO = 0.95
EPSILON = 1e-08
NESTEROV = 0.9
OUTER_RATE = 0.7
MESH = pl.DeviceIdType.MESH
BF16 = jnp.bfloat16
F32 = jnp.float32

NX, NL, NY, NH, NC = 4, 4, 4, 4, 2
ORDER = (2, 1, 3, 0)


def exchange_kernel(
    grad, proj, first_in, second_in, momentum_in, out, avg_out,
    gv, pv, fm, sm, mom, part, rsbuf, half, corebuf, ybuf, hbuf, og, av,
    load_sem, rs_send, rs_recv, core_sem, y_send, y_recv, h_send, h_recv, ag_send, ag_recv, fw_send, fw_recv, av_sem, out_sem,
):
    rows = fm.shape[1]
    hrows = rows // 2
    tensor = lax.axis_index("tensor")
    island = lax.axis_index("island")
    mx, ml = lax.rem(tensor, NX), lax.div(tensor, NX)
    mc = lax.rem(island, NC)
    my = lax.rem(lax.div(island, NC), NY)
    mh = lax.div(island, NC * NY)
    other = 1 - mc

    def tensor_at(dl, dx):
        return lax.rem(ml + dl, NL) * NX + lax.rem(mx + dx, NX)

    def island_at(dh, dy):
        return (lax.rem(mh + dh, NH) * NY + lax.rem(my + dy, NY)) * NC + mc

    sibling = (island - mc + other, tensor)
    tensor_offsets = [(dl, dx) for dl in ORDER for dx in range(NX) if (dl, dx) != (0, 0)]

    loads = [pltpu.make_async_copy(grad.at[0], gv, load_sem.at[0])]
    for j, dl in enumerate(ORDER):
        block = lax.rem(ml + dl, NL)
        width = NX * rows
        loads.append(pltpu.make_async_copy(proj.at[:, pl.ds(pl.multiple_of(block * width, width), width)], pv.at[j], load_sem.at[1 + j]))
    loads.append(pltpu.make_async_copy(first_in, fm, load_sem.at[5]))
    loads.append(pltpu.make_async_copy(second_in, sm, load_sem.at[6]))
    loads.append(pltpu.make_async_copy(momentum_in.at[pl.ds(pl.multiple_of(mc * hrows, hrows), hrows)], mom, load_sem.at[7]))
    for copy in loads:
        copy.start()

    barrier = pltpu.get_barrier_semaphore()
    partners = [(island, tensor_at(dl, dx)) for dl, dx in tensor_offsets]
    partners.append(sibling)
    partners += [(island_at(0, d), tensor) for d in range(1, NY)]
    partners += [(island_at(d, 0), tensor) for d in range(1, NH)]
    for partner in partners:
        pl.semaphore_signal(barrier, inc=1, device_id=partner, device_id_type=MESH)

    sends = []
    loads[0].wait()
    for j, dl in enumerate(ORDER):
        loads[1 + j].wait()
        block = lax.dot_general(pv[j], gv[...], (((0,), (0,)), ((), ())), preferred_element_type=F32)
        part[j] = block.astype(BF16).reshape(NX, rows, block.shape[1])
        if j == 0:
            pl.semaphore_wait(barrier, len(partners))
        for dx in range(NX):
            if (dl, dx) == (0, 0):
                continue
            k = dl * NX + dx
            copy = pltpu.make_async_remote_copy(
                src_ref=part.at[j, lax.rem(mx + dx, NX)], dst_ref=rsbuf.at[k],
                send_sem=rs_send.at[k], recv_sem=rs_recv.at[k],
                device_id=(island, tensor_at(dl, dx)), device_id_type=MESH)
            copy.start()
            sends.append(copy)
    total = part[len(ORDER) - 1, mx].astype(F32)
    for k, copy in enumerate(sends):
        dl, dx = tensor_offsets[k]
        copy.wait_recv()
        total = total + rsbuf[dl * NX + dx].astype(F32)

    loads[5].wait()
    loads[6].wait()
    first = BETA_ONE * fm[0] + (1.0 - BETA_ONE) * total
    second = BETA_TWO * sm[0] + (1.0 - BETA_TWO) * total * total
    pseudo = first / (jnp.sqrt(second) + EPSILON)
    half[0] = pseudo[:hrows]
    half[1] = pseudo[hrows:]

    copy = pltpu.make_async_remote_copy(
        src_ref=half.at[other], dst_ref=corebuf, send_sem=core_sem.at[0], recv_sem=core_sem.at[1],
        device_id=sibling, device_id_type=MESH)
    copy.start()
    sends.append(copy)
    copy.wait_recv()
    summed = half[mc] + corebuf[...]

    for buf, send, recv, n, me, at in (
        (ybuf, y_send, y_recv, NY, my, lambda d: island_at(0, d)),
        (hbuf, h_send, h_recv, NH, mh, lambda d: island_at(d, 0)),
    ):
        buf[me] = summed.astype(BF16)
        copies = []
        for d in (2, 1, 3):
            copy = pltpu.make_async_remote_copy(
                src_ref=buf.at[me], dst_ref=buf.at[me], send_sem=send.at[d], recv_sem=recv.at[d],
                device_id=(at(d), tensor), device_id_type=MESH)
            copy.start()
            copies.append(copy)
        for copy in copies:
            copy.wait_recv()
        sends += copies
        summed = buf[0].astype(F32)
        for d in range(1, n):
            summed = summed + buf[d].astype(F32)

    averaged = summed / (NH * NY * NC)
    loads[7].wait()
    velocity = NESTEROV * mom[...] + averaged
    og[tensor, mc] = (averaged + NESTEROV * velocity).astype(BF16)
    av[mc] = velocity

    gathers = []
    for dl, dx in tensor_offsets:
        k = dl * NX + dx
        copy = pltpu.make_async_remote_copy(
            src_ref=og.at[tensor, mc], dst_ref=og.at[tensor, mc], send_sem=ag_send.at[k], recv_sem=ag_recv.at[k],
            device_id=(island, tensor_at(dl, dx)), device_id_type=MESH)
        copy.start()
        gathers.append(copy)
    forwards = [
        pltpu.make_async_remote_copy(
            src_ref=av.at[mc], dst_ref=av.at[mc], send_sem=av_sem.at[0], recv_sem=av_sem.at[1],
            device_id=sibling, device_id_type=MESH),
        pltpu.make_async_remote_copy(
            src_ref=og.at[tensor, mc], dst_ref=og.at[tensor, mc], send_sem=fw_send.at[0], recv_sem=fw_recv.at[0],
            device_id=sibling, device_id_type=MESH),
    ]
    for copy in forwards:
        copy.start()
    for copy, (dl, dx) in zip(gathers, tensor_offsets):
        copy.wait_recv()
        source = tensor_at(NL - dl, NX - dx)
        k = dl * NX + dx
        forward = pltpu.make_async_remote_copy(
            src_ref=og.at[source, mc], dst_ref=og.at[source, mc], send_sem=fw_send.at[k], recv_sem=fw_recv.at[k],
            device_id=sibling, device_id_type=MESH)
        forward.start()
        forwards.append(forward)
    for copy in forwards:
        copy.wait_recv()
    stores = [pltpu.make_async_copy(og, out, out_sem.at[0]), pltpu.make_async_copy(av, avg_out, out_sem.at[1])]
    for copy in stores:
        copy.start()
    for copy in sends + gathers + forwards:
        copy.wait_send()
    for copy in stores:
        copy.wait()


def update_kernel(proj, step, update):
    update[...] = (OUTER_RATE * jnp.dot(proj[...], step[...], preferred_element_type=F32)).astype(BF16)


def local(grad_slab, projector, first_moment, second_moment, momentum):
    ff, ranks = projector.shape
    cols = grad_slab.shape[2]
    rows = first_moment.shape[1]
    hrows = rows // 2
    n = NX * NL
    any_spec = pl.BlockSpec(memory_space=pl.ANY)
    dma = pltpu.SemaphoreType.DMA
    step, velocity = pl.pallas_call(
        exchange_kernel,
        name="exchange",
        out_shape=(jax.ShapeDtypeStruct((n, NC, hrows, cols), BF16), jax.ShapeDtypeStruct((NC, hrows, cols), F32)),
        in_specs=[any_spec] * 5,
        out_specs=(any_spec, any_spec),
        scratch_shapes=[
            pltpu.VMEM((ff, cols), BF16),
            pltpu.VMEM((NL, ff, NX * rows), BF16),
            pltpu.VMEM((1, rows, cols), F32),
            pltpu.VMEM((1, rows, cols), F32),
            pltpu.VMEM((hrows, cols), F32),
            pltpu.VMEM((NL, NX, rows, cols), BF16),
            pltpu.VMEM((n, rows, cols), BF16),
            pltpu.VMEM((NC, hrows, cols), F32),
            pltpu.VMEM((hrows, cols), F32),
            pltpu.VMEM((NY, hrows, cols), BF16),
            pltpu.VMEM((NH, hrows, cols), BF16),
            pltpu.VMEM((n, NC, hrows, cols), BF16),
            pltpu.VMEM((NC, hrows, cols), F32),
            dma((8,)), dma((n,)), dma((n,)), dma((2,)), dma((NY,)), dma((NY,)), dma((NH,)), dma((NH,)),
            dma((n,)), dma((n,)), dma((n,)), dma((n,)), dma((2,)), dma((2,)),
        ],
        compiler_params=pltpu.CompilerParams(collective_id=1, has_side_effects=True, vmem_limit_bytes=24 << 20),
    )(grad_slab, projector, first_moment, second_moment, momentum)
    block = 448
    update = pl.pallas_call(
        update_kernel,
        name="update",
        grid=(ff // block,),
        out_shape=jax.ShapeDtypeStruct((ff, cols), BF16),
        in_specs=[pl.BlockSpec((block, ranks), lambda i: (i, 0)), pl.BlockSpec((ranks, cols), lambda i: (0, 0))],
        out_specs=pl.BlockSpec((block, cols), lambda i: (i, 0)),
        compiler_params=pltpu.CompilerParams(vmem_limit_bytes=16 << 20),
    )(projector, step.reshape(ranks, cols))
    return (update, velocity.reshape(rows, cols))


def solution(mesh):
    in_specs = (
        P("island", "tensor", None),
        P("tensor", None),
        P("island", "tensor", None),
        P("island", "tensor", None),
        P("tensor", None),
    )
    out_specs = (P("tensor", None), P("tensor", None))
    return jax.shard_map(local, mesh=mesh, in_specs=in_specs, out_specs=out_specs, check_vma=False)
```

time: 410 us -> 56.4 us (0.14)
  the two profiles are of different devices: /device:TPU:128 before, /device:TPU:1 now
where the time goes in v1:
time: 56.4 us; the launch traced here: 56 us
  Pallas kernels  49.5 us (88%)
  local copies, waits for them, and re-layouts  5.84 us (10%)
  between operations  0.65 us (1%)
    pallas_call x1, Pallas kernels, local(): pl.pallas_call(exchange_kernel, name='exchange', out_shape=(jax.ShapeDtyp...  46.8 us
    unnamed x11, local copies, waits for them, and re-layouts  5.84 us
    pallas_call x1, Pallas kernels, local(): pl.pallas_call(update_kernel, name='update', grid=(ff // block,), out_sha...  2.71 us

profile of v1, /device:TPU:1, one launch (start us, length us, event | category | flops | bytes accessed | tf_op | source)
XLA Modules:
  0.0 56.0 jit_solution(6388155441208837687)
XLA Ops:
  0.6 0.0 copy-start
  0.6 1.5 %copy-done = bf16[1792,512]{1,0:T(8,128)(2,1)S(1)} copy-done((bf16[1792,512]{1,0:T(8,128)(2,1)S(1)}, bf16[1792,512]{1,0:T(8,128)(2,1)}, u32[]{:S(2)}) %copy-start) | copy-done | bytes 1835032
  2.1 0.0 copy-start.1
  2.1 1.3 %copy-done.1 = bf16[1,1792,384]{2,1,0:T(8,128)(2,1)S(1)} copy-done((bf16[1,1792,384]{2,1,0:T(8,128)(2,1)S(1)}, bf16[1,1792,384]{2,1,0:T(8,128)(2,1)}, u32[]{:S(2)}) %copy-start.1) | copy-done | bytes 1376280
  3.5 0.0 copy-start.2
  3.5 0.8 %copy-done.2 = f32[1,32,384]{2,1,0:T(8,128)S(1)} copy-done((f32[1,32,384]{2,1,0:T(8,128)S(1)}, f32[1,32,384]{2,1,0:T(8,128)}, u32[]{:S(2)}) %copy-start.2) | copy-done | bytes 49176
  4.3 0.0 copy-start.3
  4.3 0.8 %copy-done.3 = f32[1,32,384]{2,1,0:T(8,128)S(1)} copy-done((f32[1,32,384]{2,1,0:T(8,128)S(1)}, f32[1,32,384]{2,1,0:T(8,128)}, u32[]{:S(2)}) %copy-start.3) | copy-done | bytes 49176
  5.1 0.0 copy-start.4
  5.1 0.8 %copy-done.4 = f32[32,384]{1,0:T(8,128)S(1)} copy-done((f32[32,384]{1,0:T(8,128)S(1)}, f32[32,384]{1,0:T(8,128)}, u32[]{:S(2)}) %copy-start.4) | copy-done | bytes 49176
  5.9 46.8 %exchange.1 = (bf16[16,2,16,384]{3,2,1,0:T(8,128)(2,1)S(1)}, f32[2,16,384]{2,1,0:T(8,128)S(1)}) custom-call(bf16[1,1792,384]{2,1,0:T(8,128)(2,1)S(1)} %copy-done.1, bf16[1792,512]{1,0:T(8,128)(2,1)S(1)} %copy-done, f32[1,32,384]{2,1,0:T(8,128)S(1)} %copy-done.2, f32[1,32,384]{2,1,0:T(8,128)S(1)} %copy-done.3, f32[32,384]{1,0:T(8,128)S(1)} %copy-done.4), custom_call_target="tpu_custom_call" | custom-call | tf_op jit(solution)/shard_map/exchange/pallas_call | solution.py:181
  52.7 2.7 %update.1 = bf16[1792,384]{1,0:T(8,128)(2,1)} custom-call(bf16[1792,512]{1,0:T(8,128)(2,1)S(1)} %copy-done, bf16[512,384]{1,0:T(8,128)(2,1)S(1)} %bitcast.2), custom_call_target="tpu_custom_call" | custom-call | tf_op jit(solution)/shard_map/update/pallas_call | solution.py:207
  55.4 0.6 %copy.8 = f32[32,384]{1,0:T(8,128)} copy(f32[32,384]{1,0:T(8,128)S(1)} %bitcast.3) | data formatting | bytes 98304
Async XLA Ops:
  0.6 1.5 %copy-start = (bf16[1792,512]{1,0:T(8,128)(2,1)S(1)}, bf16[1792,512]{1,0:T(8,128)(2,1)}, u32[]{:S(2)}) copy-start(bf16[1792,512]{1,0:T(8,128)(2,1)} %proj.3) | copy-start | bytes 5505028
  2.1 1.3 %copy-start.1 = (bf16[1,1792,384]{2,1,0:T(8,128)(2,1)S(1)}, bf16[1,1792,384]{2,1,0:T(8,128)(2,1)}, u32[]{:S(2)}) copy-start(bf16[1,1792,384]{2,1,0:T(8,128)(2,1)} %grad.1) | copy-start | bytes 4128772
  3.5 0.8 %copy-start.2 = (f32[1,32,384]{2,1,0:T(8,128)S(1)}, f32[1,32,384]{2,1,0:T(8,128)}, u32[]{:S(2)}) copy-start(f32[1,32,384]{2,1,0:T(8,128)} %first_in.1) | copy-start | bytes 147460
  4.3 0.8 %copy-start.3 = (f32[1,32,384]{2,1,0:T(8,128)S(1)}, f32[1,32,384]{2,1,0:T(8,128)}, u32[]{:S(2)}) copy-start(f32[1,32,384]{2,1,0:T(8,128)} %second_in.1) | copy-start | bytes 147460
  5.1 0.8 %copy-start.4 = (f32[32,384]{1,0:T(8,128)S(1)}, f32[32,384]{1,0:T(8,128)}, u32[]{:S(2)}) copy-start(f32[32,384]{1,0:T(8,128)} %momentum_in.1) | copy-start | bytes 147460

commit v2 on v0

v2 whole, which is shorter than its diff:
```python
import jax
import jax.numpy as jnp
from jax import lax
from jax.experimental import pallas as pl
from jax.experimental.pallas import tpu as pltpu
from jax.sharding import PartitionSpec as P

BETA_ONE = 0.9
BETA_TWO = 0.95
EPSILON = 1e-08
NESTEROV = 0.9
OUTER_RATE = 0.7
MESH = pl.DeviceIdType.MESH
BF16 = jnp.bfloat16
F32 = jnp.float32

NX, NL, NY, NH, NC = 4, 4, 4, 4, 2
NZ = NH * NL
LPC = NL // NC
ORDER = (2, 1, 3, 0)


def exchange_kernel(
    grad, proj, first_in, second_in, momentum_in, step_out, velocity_out,
    gv, pv, fm, sm, part, xbuf, lsend, lbuf, pse, ybuf, chunk, zbuf, mombuf, vel, vout, og,
    load_sem, x_send, x_recv, l_send, l_recv, y_send, y_recv, m_send, m_recv, z_send, z_recv,
    v_send, v_recv, g_send, g_recv, f_send, f_recv, out_sem,
):
    rows = fm.shape[1]
    group = rows // NY
    width = NX * rows
    tensor = lax.axis_index("tensor")
    island = lax.axis_index("island")
    mx, ml = lax.rem(tensor, NX), lax.div(tensor, NX)
    mc = lax.rem(island, NC)
    my = lax.rem(lax.div(island, NC), NY)
    mh = lax.div(island, NC * NY)
    mz = mh * NL + ml
    sigma = lax.div(ml, LPC)
    active = mc == sigma
    li = lax.rem(ml, LPC)

    def device(x=mx, y=my, z=mz, c=mc):
        return ((lax.div(z, NL) * NY + y) * NC + c, lax.rem(z, NL) * NX + x)

    def at_x(d):
        return lax.rem(mx + d, NX)

    def at_y(d):
        return lax.rem(my + d, NY)

    def at_l(d):
        return lax.rem(ml + d, NL)

    def at_z(d):
        return lax.rem(mz + d, NZ)

    sibling = device(c=1 - mc)
    xy_offsets = [(dx, dy) for dx in (2, 1, 3, 0) for dy in (2, 1, 3, 0) if (dx, dy) != (0, 0)]
    z_offsets = (8, 7, 9, 6, 10, 5, 11, 4, 12, 3, 13, 2, 14, 1, 15)

    def remote(src, dst, send, recv, to):
        return pltpu.make_async_remote_copy(
            src_ref=src, dst_ref=dst, send_sem=send, recv_sem=recv, device_id=to, device_id_type=MESH)

    loads = [pltpu.make_async_copy(grad.at[0], gv, load_sem.at[0])]
    for j, d in enumerate(ORDER):
        ranks = pl.ds(pl.multiple_of(at_l(d) * width, width), width)
        loads.append(pltpu.make_async_copy(proj.at[:, ranks], pv.at[j], load_sem.at[1 + j]))
    loads.append(pltpu.make_async_copy(first_in, fm, load_sem.at[5]))
    loads.append(pltpu.make_async_copy(second_in, sm, load_sem.at[6]))
    own_rows = pl.ds(pl.multiple_of(my * group, group), group)
    loads.append(pltpu.make_async_copy(momentum_in.at[own_rows], vel.at[0], load_sem.at[7]))
    for copy in loads:
        copy.start()

    barrier = pltpu.get_barrier_semaphore()
    partners = [device(z=at_z(d)) for d in z_offsets]
    partners += [device(x=at_x(dx), y=at_y(dy)) for dx, dy in xy_offsets]
    partners += [device(y=at_y(d), c=1 - mc) for d in range(NY)]
    for partner in partners:
        pl.semaphore_signal(barrier, inc=1, device_id=partner, device_id_type=MESH)

    x_copies = []
    loads[0].wait()
    for j, d in enumerate(ORDER):
        loads[1 + j].wait()
        block = lax.dot_general(pv[j], gv[...], (((0,), (0,)), ((), ())), preferred_element_type=F32)
        part[j] = block.astype(BF16).reshape(NX, rows, block.shape[1])
        if j == 0:
            pl.semaphore_wait(barrier, len(partners))
        for dx in (2, 1, 3):
            copy = remote(part.at[j, at_x(dx)], xbuf.at[j, dx - 1], x_send.at[j, dx - 1], x_recv.at[j, dx - 1], device(x=at_x(dx)))
            copy.start()
            x_copies.append(copy)

    loads[7].wait()
    vel[1] = vel[0]

    @pl.when(active)
    def _():
        pltpu.make_async_copy(vel.at[1], mombuf.at[li], m_recv.at[li]).start()
        for d in range(1, NL):
            remote(vel.at[1], mombuf.at[li], m_send.at[d], m_recv.at[li], device(z=mz - ml + at_l(d))).start()

    l_copies = []
    total = None
    for j, d in enumerate(ORDER):
        for k in range(3):
            x_copies[3 * j + k].wait_recv()
        total = part[j, mx].astype(F32)
        for k in range(3):
            total = total + xbuf[j, k].astype(F32)
        if d:
            lsend[j] = total.astype(BF16)
            copy = remote(lsend.at[j], lbuf.at[j], l_send.at[j], l_recv.at[j], device(z=mz - ml + at_l(d)))
            copy.start()
            l_copies.append(copy)
    loads[5].wait()
    loads[6].wait()
    for j in range(NL - 1):
        l_copies[j].wait_recv()
        total = total + lbuf[j].astype(F32)

    first = BETA_ONE * fm[0] + (1.0 - BETA_ONE) * total
    second = BETA_TWO * sm[0] + (1.0 - BETA_TWO) * total * total
    pseudo = first / (jnp.sqrt(second) + EPSILON)
    pse[...] = pseudo.reshape(pse.shape)

    slot = mc * NY + my
    y_copies = []
    for d in (2, 1, 3):
        copy = remote(pse.at[at_y(d)], ybuf.at[slot], y_send.at[d], y_recv.at[slot], device(y=at_y(d), c=sigma))
        copy.start()
        y_copies.append(copy)
    to_sibling = remote(pse.at[my], ybuf.at[slot], y_send.at[0], y_recv.at[slot], sibling)

    @pl.when(jnp.logical_not(active))
    def _():
        to_sibling.start()

    @pl.when(active)
    def _():
        pltpu.make_async_copy(pse.at[my], ybuf.at[slot], y_recv.at[slot]).start()
        for s in range(NC * NY):
            pltpu.make_async_copy(pse.at[0], ybuf.at[s], y_recv.at[s]).wait()
        summed = ybuf[0]
        for s in range(1, NC * NY):
            summed = summed + ybuf[s]
        chunk[...] = summed.astype(BF16)
        for k, d in enumerate(z_offsets):
            remote(chunk, zbuf.at[mh, li], z_send.at[k], z_recv.at[mh, li], device(z=at_z(d))).start()
        pltpu.make_async_copy(chunk, zbuf.at[mh, li], z_recv.at[mh, li]).start()

    for i in range(LPC):
        pltpu.make_async_copy(vel.at[1], mombuf.at[i], m_recv.at[i]).wait()
    for h in range(NH):
        for i in range(LPC):
            pltpu.make_async_copy(chunk, zbuf.at[h, i], z_recv.at[h, i]).wait()
    summed = zbuf[0].astype(F32)
    for h in range(1, NH):
        summed = summed + zbuf[h].astype(F32)
    averaged = summed / (NH * NY * NC)
    velocity = NESTEROV * mombuf[...] + averaged
    outer_step = (averaged + NESTEROV * velocity).astype(BF16)
    half = pl.ds(mc * LPC, LPC)
    og[half, mx, my] = outer_step
    vel[2:] = velocity

    g_copies = []
    for k, (dx, dy) in enumerate(xy_offsets):
        copy = remote(og.at[half, mx, my], og.at[half, mx, my], g_send.at[k], g_recv.at[k], device(x=at_x(dx), y=at_y(dy)))
        copy.start()
        g_copies.append(copy)
    f_copies = [remote(og.at[half, mx, my], og.at[half, mx, my], f_send.at[NX * NY - 1], f_recv.at[NX * NY - 1], sibling)]
    f_copies[0].start()

    @pl.when(active)
    def _():
        pltpu.make_async_copy(vel.at[2 + li], vout.at[my], v_recv.at[my]).start()
        for d in range(1, NY):
            for c in range(NC):
                remote(vel.at[2 + li], vout.at[my], v_send.at[d, c], v_recv.at[my], device(y=at_y(d), c=c)).start()
        remote(vel.at[2 + li], vout.at[my], v_send.at[0, 0], v_recv.at[my], sibling).start()

    for k, (dx, dy) in enumerate(xy_offsets):
        g_copies[k].wait_recv()
        src = og.at[half, at_x(NX - dx), at_y(NY - dy)]
        copy = remote(src, src, f_send.at[k], f_recv.at[k], sibling)
        copy.start()
        f_copies.append(copy)
    for copy in f_copies:
        copy.wait_recv()
    for y in range(NY):
        pltpu.make_async_copy(vel.at[2], vout.at[y], v_recv.at[y]).wait()
    stores = [pltpu.make_async_copy(og, step_out, out_sem.at[0]), pltpu.make_async_copy(vout, velocity_out, out_sem.at[1])]
    for copy in stores:
        copy.start()
    for copy in x_copies + l_copies + y_copies + g_copies + f_copies:
        copy.wait_send()

    @pl.when(jnp.logical_not(active))
    def _():
        to_sibling.wait_send()

    @pl.when(active)
    def _():
        for d in range(1, NL):
            remote(vel.at[1], mombuf.at[li], m_send.at[d], m_recv.at[li], sibling).wait_send()
        for k in range(NZ - 1):
            remote(chunk, zbuf.at[mh, li], z_send.at[k], z_recv.at[mh, li], sibling).wait_send()
        for d in range(1, NY):
            for c in range(NC):
                remote(vel.at[2], vout.at[my], v_send.at[d, c], v_recv.at[my], sibling).wait_send()
        remote(vel.at[2], vout.at[my], v_send.at[0, 0], v_recv.at[my], sibling).wait_send()

    for copy in stores:
        copy.wait()


def update_kernel(proj, step, update):
    update[...] = (OUTER_RATE * jnp.dot(proj[...], step[...], preferred_element_type=F32)).astype(BF16)


def exchange(grad_slab, projector, first_moment, second_moment, momentum):
    ff = projector.shape[0]
    cols = grad_slab.shape[2]
    rows = first_moment.shape[1]
    group = rows // NY
    any_spec = pl.BlockSpec(memory_space=pl.ANY)
    hbm_spec = pl.BlockSpec(memory_space=pltpu.HBM)
    dma = pltpu.SemaphoreType.DMA
    return pl.pallas_call(
        exchange_kernel,
        name="exchange",
        out_shape=(
            jax.ShapeDtypeStruct((NL, NX, NY, group, cols), BF16),
            jax.ShapeDtypeStruct((NY, group, cols), F32),
        ),
        in_specs=[hbm_spec] * 5,
        out_specs=(any_spec, any_spec),
        scratch_shapes=[
            pltpu.VMEM((ff, cols), BF16),
            pltpu.VMEM((NL, ff, NX * rows), BF16),
            pltpu.VMEM((1, rows, cols), F32),
            pltpu.VMEM((1, rows, cols), F32),
            pltpu.VMEM((NL, NX, rows, cols), BF16),
            pltpu.VMEM((NL, NX - 1, rows, cols), BF16),
            pltpu.VMEM((NL - 1, rows, cols), BF16),
            pltpu.VMEM((NL - 1, rows, cols), BF16),
            pltpu.VMEM((NY, group, cols), F32),
            pltpu.VMEM((NC * NY, group, cols), F32),
            pltpu.VMEM((group, cols), BF16),
            pltpu.VMEM((NH, LPC, group, cols), BF16),
            pltpu.VMEM((LPC, group, cols), F32),
            pltpu.VMEM((2 + LPC, group, cols), F32),
            pltpu.VMEM((NY, group, cols), F32),
            pltpu.VMEM((NL, NX, NY, group, cols), BF16),
            dma((8,)),
            dma((NL, NX - 1)), dma((NL, NX - 1)),
            dma((NL - 1,)), dma((NL - 1,)),
            dma((NY,)), dma((NC * NY,)),
            dma((NL,)), dma((LPC,)),
            dma((NZ - 1,)), dma((NH, LPC)),
            dma((NY, NC)), dma((NY,)),
            dma((NX * NY - 1,)), dma((NX * NY - 1,)),
            dma((NX * NY,)), dma((NX * NY,)),
            dma((2,)),
        ],
        compiler_params=pltpu.CompilerParams(collective_id=1, has_side_effects=True, vmem_limit_bytes=24 << 20),
    )(*[pltpu.with_memory_space_constraint(a, pltpu.HBM) for a in (grad_slab, projector, first_moment, second_moment, momentum)])


def local(grad_slab, projector, first_moment, second_moment, momentum):
    ff, ranks = projector.shape
    cols = grad_slab.shape[2]
    rows = first_moment.shape[1]
    step, velocity = exchange(grad_slab, projector, first_moment, second_moment, momentum)
    block = 448
    update = pl.pallas_call(
        update_kernel,
        name="update",
        grid=(ff // block,),
        out_shape=jax.ShapeDtypeStruct((ff, cols), BF16),
        in_specs=[pl.BlockSpec((block, ranks), lambda i: (i, 0)), pl.BlockSpec((ranks, cols), lambda i: (0, 0))],
        out_specs=pl.BlockSpec((block, cols), lambda i: (i, 0)),
        compiler_params=pltpu.CompilerParams(vmem_limit_bytes=16 << 20),
    )(projector, step.reshape(ranks, cols))
    return (update, velocity.reshape(rows, cols))


def solution(mesh):
    in_specs = (
        P("island", "tensor", None),
        P("tensor", None),
        P("island", "tensor", None),
        P("island", "tensor", None),
        P("tensor", None),
    )
    out_specs = (P("tensor", None), P("tensor", None))
    return jax.shard_map(local, mesh=mesh, in_specs=in_specs, out_specs=out_specs, check_vma=False)
```

time: 410 us -> 47.9 us (0.12)
  the two profiles are of different devices: /device:TPU:128 before, /device:TPU:1 now
where the time goes in v2:
time: 47.9 us; the launch traced here: 47.8 us
  Pallas kernels  46.5 us (97%)
  between operations  0.66 us (1%)
  local copies, waits for them, and re-layouts  0.62 us (1%)
    pallas_call x1, Pallas kernels, exchange(): pl.pallas_call(exchange_kernel, name='exchange', out_shape=(jax.ShapeDtyp...  43.8 us
    pallas_call x1, Pallas kernels, local(): pl.pallas_call(update_kernel, name='update', grid=(ff // block,), out_sha...  2.71 us

profile of v2, /device:TPU:1, one launch (start us, length us, event | category | flops | bytes accessed | tf_op | source)
XLA Modules:
  0.0 47.8 jit_solution(6959974541967420740)
XLA Ops:
  0.6 0.0 copy-start
  0.6 43.8 %exchange.1 = (bf16[4,4,4,8,384]{4,3,2,1,0:T(8,128)(2,1)S(1)}, f32[4,8,384]{2,1,0:T(8,128)S(1)}) custom-call(bf16[1,1792,384]{2,1,0:T(8,128)(2,1)} %grad.1, bf16[1792,512]{1,0:T(8,128)(2,1)} %proj.3, f32[1,32,384]{2,1,0:T(8,128)} %first_in.1, f32[1,32,384]{2,1,0:T(8,128)} %second_in.1, f32[32,384]{1,0:T(8,128)} %momentum_in.1), custom_call_target="tpu_custom_call" | custom-call | tf_op jit(solution)/shard_map/exchange/pallas_call | solution.py:233
  44.5 0.0 copy-done
  44.5 2.7 %update.1 = bf16[1792,384]{1,0:T(8,128)(2,1)} custom-call(bf16[1792,512]{1,0:T(8,128)(2,1)S(1)} %copy-done, bf16[512,384]{1,0:T(8,128)(2,1)S(1)} %bitcast.2), custom_call_target="tpu_custom_call" | custom-call | tf_op jit(solution)/shard_map/update/pallas_call | solution.py:280
  47.2 0.6 %copy.8 = f32[32,384]{1,0:T(8,128)} copy(f32[32,384]{1,0:T(8,128)S(1)} %bitcast.3) | data formatting | bytes 98304
Async XLA Ops:
  0.6 43.8 %copy-start = (bf16[1792,512]{1,0:T(8,128)(2,1)S(1)}, bf16[1792,512]{1,0:T(8,128)(2,1)}, u32[]{:S(2)}) copy-start(bf16[1792,512]{1,0:T(8,128)(2,1)} %proj.3) | copy-start | bytes 5505028

commit v3 on v2

--- a/solution.py
+++ b/solution.py
@@ -17,14 +17,15 @@
 NX, NL, NY, NH, NC = 4, 4, 4, 4, 2
 NZ = NH * NL
 LPC = NL // NC
-ORDER = (2, 1, 3, 0)
+REACH = 4
+UPDATE_ROWS = 256
 
 
 def exchange_kernel(
-    grad, proj, first_in, second_in, momentum_in, step_out, velocity_out,
-    gv, pv, fm, sm, part, xbuf, lsend, lbuf, pse, ybuf, chunk, zbuf, mombuf, vel, vout, og,
+    grad, proj, first_in, second_in, momentum_in, pv, og, vout,
+    gv, fm, sm, part, xbuf, lsend, lbuf, pse, ybuf, chunk, zbuf, mombuf, vel,
     load_sem, x_send, x_recv, l_send, l_recv, y_send, y_recv, m_send, m_recv, z_send, z_recv,
-    v_send, v_recv, g_send, g_recv, f_send, f_recv, out_sem,
+    v_send, v_recv, g_send, g_recv, f_send, f_recv, ring_sem,
 ):
     rows = fm.shape[1]
     group = rows // NY
@@ -55,6 +56,9 @@
     def at_z(d):
         return lax.rem(mz + d, NZ)
 
+    farthest = jnp.where(ml < 2, 3, 0)
+    nearer = 1 + lax.rem(ml, 2)
+    order = (farthest, 6 - ml - farthest - nearer, nearer, ml)
     sibling = device(c=1 - mc)
     xy_offsets = [(dx, dy) for dx in (2, 1, 3, 0) for dy in (2, 1, 3, 0) if (dx, dy) != (0, 0)]
     z_offsets = (8, 7, 9, 6, 10, 5, 11, 4, 12, 3, 13, 2, 14, 1, 15)
@@ -64,9 +68,9 @@
             src_ref=src, dst_ref=dst, send_sem=send, recv_sem=recv, device_id=to, device_id_type=MESH)
 
     loads = [pltpu.make_async_copy(grad.at[0], gv, load_sem.at[0])]
-    for j, d in enumerate(ORDER):
-        ranks = pl.ds(pl.multiple_of(at_l(d) * width, width), width)
-        loads.append(pltpu.make_async_copy(proj.at[:, ranks], pv.at[j], load_sem.at[1 + j]))
+    ranks = [pl.ds(pl.multiple_of(block * width, width), width) for block in order]
+    for j in range(NL):
+        loads.append(pltpu.make_async_copy(proj.at[:, ranks[j]], pv.at[:, ranks[j]], load_sem.at[1 + j]))
     loads.append(pltpu.make_async_copy(first_in, fm, load_sem.at[5]))
     loads.append(pltpu.make_async_copy(second_in, sm, load_sem.at[6]))
     own_rows = pl.ds(pl.multiple_of(my * group, group), group)
@@ -75,7 +79,7 @@
         copy.start()
 
     barrier = pltpu.get_barrier_semaphore()
-    partners = [device(z=at_z(d)) for d in z_offsets]
+    partners = [device(z=at_z(d)) for d in z_offsets if min(d, NZ - d) <= REACH]
     partners += [device(x=at_x(dx), y=at_y(dy)) for dx, dy in xy_offsets]
     partners += [device(y=at_y(d), c=1 - mc) for d in range(NY)]
     for partner in partners:
@@ -83,12 +87,14 @@
 
     x_copies = []
     loads[0].wait()
-    for j, d in enumerate(ORDER):
+    for j in range(NL):
         loads[1 + j].wait()
-        block = lax.dot_general(pv[j], gv[...], (((0,), (0,)), ((), ())), preferred_element_type=F32)
+        block = lax.dot_general(pv[:, ranks[j]], gv[...], (((0,), (0,)), ((), ())), preferred_element_type=F32)
         part[j] = block.astype(BF16).reshape(NX, rows, block.shape[1])
         if j == 0:
             pl.semaphore_wait(barrier, len(partners))
+            for d in (REACH, NZ - REACH):
+                pl.semaphore_signal(ring_sem, inc=1, device_id=device(z=at_z(d)), device_id_type=MESH)
         for dx in (2, 1, 3):
             copy = remote(part.at[j, at_x(dx)], xbuf.at[j, dx - 1], x_send.at[j, dx - 1], x_recv.at[j, dx - 1], device(x=at_x(dx)))
             copy.start()
@@ -105,22 +111,22 @@
 
     l_copies = []
     total = None
-    for j, d in enumerate(ORDER):
+    for j in range(NL):
         for k in range(3):
             x_copies[3 * j + k].wait_recv()
         total = part[j, mx].astype(F32)
         for k in range(3):
             total = total + xbuf[j, k].astype(F32)
-        if d:
+        if j < NL - 1:
             lsend[j] = total.astype(BF16)
-            copy = remote(lsend.at[j], lbuf.at[j], l_send.at[j], l_recv.at[j], device(z=mz - ml + at_l(d)))
+            copy = remote(lsend.at[j], lbuf.at[ml], l_send.at[j], l_recv.at[ml], device(z=mz - ml + order[j]))
             copy.start()
             l_copies.append(copy)
     loads[5].wait()
     loads[6].wait()
-    for j in range(NL - 1):
-        l_copies[j].wait_recv()
-        total = total + lbuf[j].astype(F32)
+    for d in range(1, NL):
+        pltpu.make_async_copy(lsend.at[0], lbuf.at[at_l(d)], l_recv.at[at_l(d)]).wait()
+        total = total + lbuf[at_l(d)].astype(F32)
 
     first = BETA_ONE * fm[0] + (1.0 - BETA_ONE) * total
     second = BETA_TWO * sm[0] + (1.0 - BETA_TWO) * total * total
@@ -138,6 +144,8 @@
     @pl.when(jnp.logical_not(active))
     def _():
         to_sibling.start()
+
+    pl.semaphore_wait(ring_sem, 2)
 
     @pl.when(active)
     def _():
@@ -193,9 +201,6 @@
         copy.wait_recv()
     for y in range(NY):
         pltpu.make_async_copy(vel.at[2], vout.at[y], v_recv.at[y]).wait()
-    stores = [pltpu.make_async_copy(og, step_out, out_sem.at[0]), pltpu.make_async_copy(vout, velocity_out, out_sem.at[1])]
-    for copy in stores:
-        copy.start()
     for copy in x_copies + l_copies + y_copies + g_copies + f_copies:
         copy.wait_send()
 
@@ -214,12 +219,19 @@
                 remote(vel.at[2], vout.at[my], v_send.at[d, c], v_recv.at[my], sibling).wait_send()
         remote(vel.at[2], vout.at[my], v_send.at[0, 0], v_recv.at[my], sibling).wait_send()
 
+
+def update_kernel(proj, step, velocity, update_out, velocity_out, update, sem):
+    blocks = proj.shape[0] // UPDATE_ROWS
+    stores = [pltpu.make_async_copy(velocity, velocity_out, sem.at[blocks])]
+    stores[0].start()
+    for i in range(blocks):
+        rows = pl.ds(i * UPDATE_ROWS, UPDATE_ROWS)
+        update[rows] = (OUTER_RATE * jnp.dot(proj[rows], step[...], preferred_element_type=F32)).astype(BF16)
+        copy = pltpu.make_async_copy(update.at[rows], update_out.at[rows], sem.at[i])
+        copy.start()
+        stores.append(copy)
     for copy in stores:
         copy.wait()
-
-
-def update_kernel(proj, step, update):
-    update[...] = (OUTER_RATE * jnp.dot(proj[...], step[...], preferred_element_type=F32)).astype(BF16)
 
 
 def exchange(grad_slab, projector, first_moment, second_moment, momentum):
@@ -227,45 +239,43 @@
     cols = grad_slab.shape[2]
     rows = first_moment.shape[1]
     group = rows // NY
-    any_spec = pl.BlockSpec(memory_space=pl.ANY)
+    vmem_spec = pl.BlockSpec(memory_space=pltpu.VMEM)
     hbm_spec = pl.BlockSpec(memory_space=pltpu.HBM)
     dma = pltpu.SemaphoreType.DMA
     return pl.pallas_call(
         exchange_kernel,
         name="exchange",
         out_shape=(
-            jax.ShapeDtypeStruct((NL, NX, NY, group, cols), BF16),
-            jax.ShapeDtypeStruct((NY, group, cols), F32),
+            pltpu.VMEM(projector.shape, BF16),
+            pltpu.VMEM((NL, NX, NY, group, cols), BF16),
+            pltpu.VMEM((NY, group, cols), F32),
         ),
         in_specs=[hbm_spec] * 5,
-        out_specs=(any_spec, any_spec),
+        out_specs=(vmem_spec,) * 3,
         scratch_shapes=[
             pltpu.VMEM((ff, cols), BF16),
-            pltpu.VMEM((NL, ff, NX * rows), BF16),
             pltpu.VMEM((1, rows, cols), F32),
             pltpu.VMEM((1, rows, cols), F32),
             pltpu.VMEM((NL, NX, rows, cols), BF16),
             pltpu.VMEM((NL, NX - 1, rows, cols), BF16),
             pltpu.VMEM((NL - 1, rows, cols), BF16),
-            pltpu.VMEM((NL - 1, rows, cols), BF16),
+            pltpu.VMEM((NL, rows, cols), BF16),
             pltpu.VMEM((NY, group, cols), F32),
             pltpu.VMEM((NC * NY, group, cols), F32),
             pltpu.VMEM((group, cols), BF16),
             pltpu.VMEM((NH, LPC, group, cols), BF16),
             pltpu.VMEM((LPC, group, cols), F32),
             pltpu.VMEM((2 + LPC, group, cols), F32),
-            pltpu.VMEM((NY, group, cols), F32),
-            pltpu.VMEM((NL, NX, NY, group, cols), BF16),
             dma((8,)),
             dma((NL, NX - 1)), dma((NL, NX - 1)),
-            dma((NL - 1,)), dma((NL - 1,)),
+            dma((NL - 1,)), dma((NL,)),
             dma((NY,)), dma((NC * NY,)),
             dma((NL,)), dma((LPC,)),
             dma((NZ - 1,)), dma((NH, LPC)),
             dma((NY, NC)), dma((NY,)),
             dma((NX * NY - 1,)), dma((NX * NY - 1,)),
             dma((NX * NY,)), dma((NX * NY,)),
-            dma((2,)),
+            pltpu.SemaphoreType.REGULAR,
         ],
         compiler_params=pltpu.CompilerParams(collective_id=1, has_side_effects=True, vmem_limit_bytes=24 << 20),
     )(*[pltpu.with_memory_space_constraint(a, pltpu.HBM) for a in (grad_slab, projector, first_moment, second_moment, momentum)])
@@ -275,18 +285,19 @@
     ff, ranks = projector.shape
     cols = grad_slab.shape[2]
     rows = first_moment.shape[1]
-    step, velocity = exchange(grad_slab, projector, first_moment, second_moment, momentum)
-    block = 448
-    update = pl.pallas_call(
+    proj, step, velocity = exchange(grad_slab, projector, first_moment, second_moment, momentum)
+    vmem_spec = pl.BlockSpec(memory_space=pltpu.VMEM)
+    any_spec = pl.BlockSpec(memory_space=pl.ANY)
+    operands = (proj, step.reshape(ranks, cols), velocity.reshape(rows, cols))
+    return pl.pallas_call(
         update_kernel,
         name="update",
-        grid=(ff // block,),
-        out_shape=jax.ShapeDtypeStruct((ff, cols), BF16),
-        in_specs=[pl.BlockSpec((block, ranks), lambda i: (i, 0)), pl.BlockSpec((ranks, cols), lambda i: (0, 0))],
-        out_specs=pl.BlockSpec((block, cols), lambda i: (i, 0)),
+        out_shape=(jax.ShapeDtypeStruct((ff, cols), BF16), jax.ShapeDtypeStruct((rows, cols), F32)),
+        in_specs=[vmem_spec] * 3,
+        out_specs=(any_spec, any_spec),
+        scratch_shapes=[pltpu.VMEM((ff, cols), BF16), pltpu.SemaphoreType.DMA((ff // UPDATE_ROWS + 1,))],
         compiler_params=pltpu.CompilerParams(vmem_limit_bytes=16 << 20),
-    )(projector, step.reshape(ranks, cols))
-    return (update, velocity.reshape(rows, cols))
+    )(*[pltpu.with_memory_space_constraint(a, pltpu.VMEM) for a in operands])
 
 
 def solution(mesh):

time: 47.9 us -> 45.5 us (0.950)
  Pallas kernels: 46.5 us -> 44.8 us
  local copies, waits for them, and re-layouts: 0.62 us -> 0 us
    pallas_call x2, Pallas kernels: 46.5 us -> 44.8 us  [the longest x1 42.9 us: exchange(): pl.pallas_call(exchange_kernel, name='exchange', out_shape=(pltpu.VMEM(pr...]
    unnamed x3 -> x0, local copies, waits for them, and re-layouts: 0.62 us -> none
where the time goes in v3:
time: 45.5 us; the launch traced here: 45.4 us
  Pallas kernels  44.8 us (98%)
  between operations  0.64 us (1%)
    pallas_call x1, Pallas kernels, exchange(): pl.pallas_call(exchange_kernel, name='exchange', out_shape=(pltpu.VMEM(pr...  42.9 us
    pallas_call x1, Pallas kernels, local(): pl.pallas_call(update_kernel, name='update', out_shape=(jax.ShapeDtypeStr...  1.86 us

profile of v3, /device:TPU:1, one launch (start us, length us, event | category | flops | bytes accessed | tf_op | source)
XLA Modules:
  0.0 45.4 jit_solution(3526977718727424667)
XLA Ops:
  0.6 42.9 %exchange.1 = (bf16[1792,512]{1,0:T(8,128)(2,1)S(1)}, bf16[4,4,4,8,384]{4,3,2,1,0:T(8,128)(2,1)S(1)}, f32[4,8,384]{2,1,0:T(8,128)S(1)}) custom-call(bf16[1,1792,384]{2,1,0:T(8,128)(2,1)} %grad.1, bf16[1792,512]{1,0:T(8,128)(2,1)} %proj.1, f32[1,32,384]{2,1,0:T(8,128)} %first_in.1, f32[1,32,384]{2,1,0:T(8,128)} %second_in.1, f32[32,384]{1,0:T(8,128)} %momentum_in.1), custom_call_target="tpu_custom_call" | custom-call | tf_op jit(solution)/shard_map/exchange/pallas_call | solution.py:245
  43.5 1.9 %update.1 = (bf16[1792,384]{1,0:T(8,128)(2,1)}, f32[32,384]{1,0:T(8,128)}) custom-call(bf16[1792,512]{1,0:T(8,128)(2,1)S(1)} %get-tuple-element.5.proj, bf16[512,384]{1,0:T(8,128)(2,1)S(1)} %bitcast.2, f32[32,384]{1,0:T(8,128)S(1)} %bitcast.3), custom_call_target="tpu_custom_call" | custom-call | tf_op jit(solution)/shard_map/update/pallas_call | solution.py:292

commit v4 on v3

--- a/solution.py
+++ b/solution.py
@@ -17,7 +17,7 @@
 NX, NL, NY, NH, NC = 4, 4, 4, 4, 2
 NZ = NH * NL
 LPC = NL // NC
-REACH = 4
+REACH = 2
 UPDATE_ROWS = 256
 
 
@@ -25,7 +25,7 @@
     grad, proj, first_in, second_in, momentum_in, pv, og, vout,
     gv, fm, sm, part, xbuf, lsend, lbuf, pse, ybuf, chunk, zbuf, mombuf, vel,
     load_sem, x_send, x_recv, l_send, l_recv, y_send, y_recv, m_send, m_recv, z_send, z_recv,
-    v_send, v_recv, g_send, g_recv, f_send, f_recv, ring_sem,
+    v_send, v_recv, g_send, g_recv, f_send, f_recv, ring_sem, wide_sem,
 ):
     rows = fm.shape[1]
     group = rows // NY
@@ -60,7 +60,9 @@
     nearer = 1 + lax.rem(ml, 2)
     order = (farthest, 6 - ml - farthest - nearer, nearer, ml)
     sibling = device(c=1 - mc)
-    xy_offsets = [(dx, dy) for dx in (2, 1, 3, 0) for dy in (2, 1, 3, 0) if (dx, dy) != (0, 0)]
+    xy_offsets = sorted(
+        [(dx, dy) for dx in range(NX) for dy in range(NY) if (dx, dy) != (0, 0)],
+        key=lambda d: -(min(d[0], NX - d[0]) + min(d[1], NY - d[1])))
     z_offsets = (8, 7, 9, 6, 10, 5, 11, 4, 12, 3, 13, 2, 14, 1, 15)
 
     def remote(src, dst, send, recv, to):
@@ -80,7 +82,8 @@
 
     barrier = pltpu.get_barrier_semaphore()
     partners = [device(z=at_z(d)) for d in z_offsets if min(d, NZ - d) <= REACH]
-    partners += [device(x=at_x(dx), y=at_y(dy)) for dx, dy in xy_offsets]
+    partners += [device(x=at_x(d)) for d in range(1, NX)]
+    partners += [device(y=at_y(d)) for d in range(1, NY)]
     partners += [device(y=at_y(d), c=1 - mc) for d in range(NY)]
     for partner in partners:
         pl.semaphore_signal(barrier, inc=1, device_id=partner, device_id_type=MESH)
@@ -90,7 +93,8 @@
     for j in range(NL):
         loads[1 + j].wait()
         block = lax.dot_general(pv[:, ranks[j]], gv[...], (((0,), (0,)), ((), ())), preferred_element_type=F32)
-        part[j] = block.astype(BF16).reshape(NX, rows, block.shape[1])
+        block = block.astype(BF16)
+        part[j] = block.reshape(part.shape[1:])
         if j == 0:
             pl.semaphore_wait(barrier, len(partners))
             for d in (REACH, NZ - REACH):
@@ -100,6 +104,10 @@
             copy.start()
             x_copies.append(copy)
 
+    pl.semaphore_wait(ring_sem, 2)
+    for d in (2 * REACH, NZ - 2 * REACH):
+        pl.semaphore_signal(wide_sem, inc=1, device_id=device(z=at_z(d)), device_id_type=MESH)
+
     loads[7].wait()
     vel[1] = vel[0]
 
@@ -109,19 +117,21 @@
         for d in range(1, NL):
             remote(vel.at[1], mombuf.at[li], m_send.at[d], m_recv.at[li], device(z=mz - ml + at_l(d))).start()
 
-    l_copies = []
-    total = None
-    for j in range(NL):
+    def over_x(j):
         for k in range(3):
             x_copies[3 * j + k].wait_recv()
         total = part[j, mx].astype(F32)
         for k in range(3):
             total = total + xbuf[j, k].astype(F32)
-        if j < NL - 1:
-            lsend[j] = total.astype(BF16)
-            copy = remote(lsend.at[j], lbuf.at[ml], l_send.at[j], l_recv.at[ml], device(z=mz - ml + order[j]))
-            copy.start()
-            l_copies.append(copy)
+        return total
+
+    l_copies = []
+    for j in range(NL - 1):
+        lsend[j] = over_x(j).astype(BF16)
+        copy = remote(lsend.at[j], lbuf.at[ml], l_send.at[j], l_recv.at[ml], device(z=mz - ml + order[j]))
+        copy.start()
+        l_copies.append(copy)
+    total = over_x(NL - 1)
     loads[5].wait()
     loads[6].wait()
     for d in range(1, NL):
@@ -145,7 +155,7 @@
     def _():
         to_sibling.start()
 
-    pl.semaphore_wait(ring_sem, 2)
+    pl.semaphore_wait(wide_sem, 2)
 
     @pl.when(active)
     def _():
@@ -159,6 +169,18 @@
         for k, d in enumerate(z_offsets):
             remote(chunk, zbuf.at[mh, li], z_send.at[k], z_recv.at[mh, li], device(z=at_z(d))).start()
         pltpu.make_async_copy(chunk, zbuf.at[mh, li], z_recv.at[mh, li]).start()
+
+    for copy in x_copies + l_copies + y_copies:
+        copy.wait_send()
+
+    @pl.when(jnp.logical_not(active))
+    def _():
+        to_sibling.wait_send()
+
+    @pl.when(active)
+    def _():
+        for d in range(1, NL):
+            remote(vel.at[1], mombuf.at[li], m_send.at[d], m_recv.at[li], sibling).wait_send()
 
     for i in range(LPC):
         pltpu.make_async_copy(vel.at[1], mombuf.at[i], m_recv.at[i]).wait()
@@ -175,13 +197,16 @@
     og[half, mx, my] = outer_step
     vel[2:] = velocity
 
-    g_copies = []
+    own = og.at[half, mx, my]
+    g_copies, f_copies = [], []
     for k, (dx, dy) in enumerate(xy_offsets):
-        copy = remote(og.at[half, mx, my], og.at[half, mx, my], g_send.at[k], g_recv.at[k], device(x=at_x(dx), y=at_y(dy)))
-        copy.start()
-        g_copies.append(copy)
-    f_copies = [remote(og.at[half, mx, my], og.at[half, mx, my], f_send.at[NX * NY - 1], f_recv.at[NX * NY - 1], sibling)]
-    f_copies[0].start()
+        g_copies.append(remote(own, own, g_send.at[k], g_recv.at[k], device(x=at_x(dx), y=at_y(dy))))
+        g_copies[k].start()
+        if k == 0:
+            f_copies.append(remote(own, own, f_send.at[k], f_recv.at[k], device(x=at_x(dx), y=at_y(dy), c=1 - mc)))
+            f_copies[0].start()
+    f_copies.append(remote(own, own, f_send.at[NX * NY - 1], f_recv.at[NX * NY - 1], sibling))
+    f_copies[1].start()
 
     @pl.when(active)
     def _():
@@ -190,34 +215,33 @@
             for c in range(NC):
                 remote(vel.at[2 + li], vout.at[my], v_send.at[d, c], v_recv.at[my], device(y=at_y(d), c=c)).start()
         remote(vel.at[2 + li], vout.at[my], v_send.at[0, 0], v_recv.at[my], sibling).start()
-
-    for k, (dx, dy) in enumerate(xy_offsets):
+        for k in range(NZ - 1):
+            remote(chunk, zbuf.at[mh, li], z_send.at[k], z_recv.at[mh, li], sibling).wait_send()
+
+    for k in reversed(range(NX * NY - 1)):
         g_copies[k].wait_recv()
-        src = og.at[half, at_x(NX - dx), at_y(NY - dy)]
-        copy = remote(src, src, f_send.at[k], f_recv.at[k], sibling)
-        copy.start()
-        f_copies.append(copy)
-    for copy in f_copies:
-        copy.wait_recv()
+        if k > 0:
+            dx, dy = xy_offsets[k]
+            src = og.at[half, at_x(NX - dx), at_y(NY - dy)]
+            copy = remote(src, src, f_send.at[k], f_recv.at[k], sibling)
+            copy.start()
+            f_copies.append(copy)
+    for copy in g_copies:
+        copy.wait_send()
     for y in range(NY):
         pltpu.make_async_copy(vel.at[2], vout.at[y], v_recv.at[y]).wait()
-    for copy in x_copies + l_copies + y_copies + g_copies + f_copies:
-        copy.wait_send()
-
-    @pl.when(jnp.logical_not(active))
-    def _():
-        to_sibling.wait_send()
-
-    @pl.when(active)
-    def _():
-        for d in range(1, NL):
-            remote(vel.at[1], mombuf.at[li], m_send.at[d], m_recv.at[li], sibling).wait_send()
-        for k in range(NZ - 1):
-            remote(chunk, zbuf.at[mh, li], z_send.at[k], z_recv.at[mh, li], sibling).wait_send()
+
+    @pl.when(active)
+    def _():
         for d in range(1, NY):
             for c in range(NC):
                 remote(vel.at[2], vout.at[my], v_send.at[d, c], v_recv.at[my], sibling).wait_send()
         remote(vel.at[2], vout.at[my], v_send.at[0, 0], v_recv.at[my], sibling).wait_send()
+
+    for copy in f_copies:
+        copy.wait_send()
+    for copy in f_copies:
+        copy.wait_recv()
 
 
 def update_kernel(proj, step, velocity, update_out, velocity_out, update, sem):
@@ -276,6 +300,7 @@
             dma((NX * NY - 1,)), dma((NX * NY - 1,)),
             dma((NX * NY,)), dma((NX * NY,)),
             pltpu.SemaphoreType.REGULAR,
+            pltpu.SemaphoreType.REGULAR,
         ],
         compiler_params=pltpu.CompilerParams(collective_id=1, has_side_effects=True, vmem_limit_bytes=24 << 20),
     )(*[pltpu.with_memory_space_constraint(a, pltpu.HBM) for a in (grad_slab, projector, first_moment, second_moment, momentum)])

time: 45.5 us -> 43.8 us (0.963)
  Pallas kernels: 44.8 us -> 43 us
    pallas_call x1, Pallas kernels: 42.9 us -> 41.1 us  [exchange(): pl.pallas_call(exchange_kernel, name='exchange', out_shape=(pltpu.VMEM(pr...]
where the time goes in v4:
time: 43.8 us; the launch traced here: 43.6 us
  Pallas kernels  43 us (98%)
  between operations  0.64 us (1%)
    pallas_call x1, Pallas kernels, exchange(): pl.pallas_call(exchange_kernel, name='exchange', out_shape=(pltpu.VMEM(pr...  41.1 us
    pallas_call x1, Pallas kernels, local(): pl.pallas_call(update_kernel, name='update', out_shape=(jax.ShapeDtypeStr...  1.86 us

profile of v4, /device:TPU:1, one launch (start us, length us, event | category | flops | bytes accessed | tf_op | source)
XLA Modules:
  0.0 43.6 jit_solution(8971068689260918030)
XLA Ops:
  0.6 41.1 %exchange.1 = (bf16[1792,512]{1,0:T(8,128)(2,1)S(1)}, bf16[4,4,4,8,384]{4,3,2,1,0:T(8,128)(2,1)S(1)}, f32[4,8,384]{2,1,0:T(8,128)S(1)}) custom-call(bf16[1,1792,384]{2,1,0:T(8,128)(2,1)} %grad.1, bf16[1792,512]{1,0:T(8,128)(2,1)} %proj.1, f32[1,32,384]{2,1,0:T(8,128)} %first_in.1, f32[1,32,384]{2,1,0:T(8,128)} %second_in.1, f32[32,384]{1,0:T(8,128)} %momentum_in.1), custom_call_target="tpu_custom_call" | custom-call | tf_op jit(solution)/shard_map/exchange/pallas_call | solution.py:269
  41.8 1.9 %update.1 = (bf16[1792,384]{1,0:T(8,128)(2,1)}, f32[32,384]{1,0:T(8,128)}) custom-call(bf16[1792,512]{1,0:T(8,128)(2,1)S(1)} %get-tuple-element.5.proj, bf16[512,384]{1,0:T(8,128)(2,1)S(1)} %bitcast.2, f32[32,384]{1,0:T(8,128)S(1)} %bitcast.3), custom_call_target="tpu_custom_call" | custom-call | tf_op jit(solution)/shard_map/update/pallas_call | solution.py:317

commit v5 on v4

--- a/solution.py
+++ b/solution.py
@@ -22,7 +22,7 @@
 
 
 def exchange_kernel(
-    grad, proj, first_in, second_in, momentum_in, pv, og, vout,
+    grad, proj, first_in, second_in, momentum_in, pv, og, vout, acc,
     gv, fm, sm, part, xbuf, lsend, lbuf, pse, ybuf, chunk, zbuf, mombuf, vel,
     load_sem, x_send, x_recv, l_send, l_recv, y_send, y_recv, m_send, m_recv, z_send, z_recv,
     v_send, v_recv, g_send, g_recv, f_send, f_recv, ring_sem, wide_sem,
@@ -62,7 +62,7 @@
     sibling = device(c=1 - mc)
     xy_offsets = sorted(
         [(dx, dy) for dx in range(NX) for dy in range(NY) if (dx, dy) != (0, 0)],
-        key=lambda d: -(min(d[0], NX - d[0]) + min(d[1], NY - d[1])))
+        key=lambda d: (d == (2, 2), -(min(d[0], NX - d[0]) + min(d[1], NY - d[1]))))
     z_offsets = (8, 7, 9, 6, 10, 5, 11, 4, 12, 3, 13, 2, 14, 1, 15)
 
     def remote(src, dst, send, recv, to):
@@ -77,8 +77,8 @@
     loads.append(pltpu.make_async_copy(second_in, sm, load_sem.at[6]))
     own_rows = pl.ds(pl.multiple_of(my * group, group), group)
     loads.append(pltpu.make_async_copy(momentum_in.at[own_rows], vel.at[0], load_sem.at[7]))
-    for copy in loads:
-        copy.start()
+    for j in (0, 1, 5, 6, 7):
+        loads[j].start()
 
     barrier = pltpu.get_barrier_semaphore()
     partners = [device(z=at_z(d)) for d in z_offsets if min(d, NZ - d) <= REACH]
@@ -90,8 +90,12 @@
 
     x_copies = []
     loads[0].wait()
+    loads[1].wait()
+    for j in range(1, NL):
+        loads[1 + j].start()
     for j in range(NL):
-        loads[1 + j].wait()
+        if j:
+            loads[1 + j].wait()
         block = lax.dot_general(pv[:, ranks[j]], gv[...], (((0,), (0,)), ((), ())), preferred_element_type=F32)
         block = block.astype(BF16)
         part[j] = block.reshape(part.shape[1:])
@@ -202,7 +206,7 @@
     for k, (dx, dy) in enumerate(xy_offsets):
         g_copies.append(remote(own, own, g_send.at[k], g_recv.at[k], device(x=at_x(dx), y=at_y(dy))))
         g_copies[k].start()
-        if k == 0:
+        if k == NX * NY - 2:
             f_copies.append(remote(own, own, f_send.at[k], f_recv.at[k], device(x=at_x(dx), y=at_y(dy), c=1 - mc)))
             f_copies[0].start()
     f_copies.append(remote(own, own, f_send.at[NX * NY - 1], f_recv.at[NX * NY - 1], sibling))
@@ -218,14 +222,18 @@
         for k in range(NZ - 1):
             remote(chunk, zbuf.at[mh, li], z_send.at[k], z_recv.at[mh, li], sibling).wait_send()
 
-    for k in reversed(range(NX * NY - 1)):
+    for k in [*reversed(range(NX * NY - 2)), NX * NY - 2]:
         g_copies[k].wait_recv()
-        if k > 0:
+        if k < NX * NY - 2:
             dx, dy = xy_offsets[k]
             src = og.at[half, at_x(NX - dx), at_y(NY - dy)]
             copy = remote(src, src, f_send.at[k], f_recv.at[k], sibling)
             copy.start()
             f_copies.append(copy)
+    near = og[half].reshape(LPC * width, og.shape[-1])
+    for i in range(acc.shape[0] // UPDATE_ROWS):
+        block = pl.ds(i * UPDATE_ROWS, UPDATE_ROWS)
+        acc[block] = jnp.dot(pv[block, pl.ds(pl.multiple_of(mc * LPC * width, LPC * width), LPC * width)], near, preferred_element_type=F32)
     for copy in g_copies:
         copy.wait_send()
     for y in range(NY):
@@ -244,13 +252,16 @@
         copy.wait_recv()
 
 
-def update_kernel(proj, step, velocity, update_out, velocity_out, update, sem):
+def update_kernel(proj, step, velocity, acc, update_out, velocity_out, update, sem):
+    ranks = step.shape[0] // NC
+    far = pl.ds(pl.multiple_of((1 - lax.rem(lax.axis_index("island"), NC)) * ranks, ranks), ranks)
+    rest = step[far]
     blocks = proj.shape[0] // UPDATE_ROWS
     stores = [pltpu.make_async_copy(velocity, velocity_out, sem.at[blocks])]
     stores[0].start()
     for i in range(blocks):
         rows = pl.ds(i * UPDATE_ROWS, UPDATE_ROWS)
-        update[rows] = (OUTER_RATE * jnp.dot(proj[rows], step[...], preferred_element_type=F32)).astype(BF16)
+        update[rows] = (OUTER_RATE * (acc[rows] + jnp.dot(proj[rows, far], rest, preferred_element_type=F32))).astype(BF16)
         copy = pltpu.make_async_copy(update.at[rows], update_out.at[rows], sem.at[i])
         copy.start()
         stores.append(copy)
@@ -273,9 +284,10 @@
             pltpu.VMEM(projector.shape, BF16),
             pltpu.VMEM((NL, NX, NY, group, cols), BF16),
             pltpu.VMEM((NY, group, cols), F32),
+            pltpu.VMEM((ff, cols), F32),
         ),
         in_specs=[hbm_spec] * 5,
-        out_specs=(vmem_spec,) * 3,
+        out_specs=(vmem_spec,) * 4,
         scratch_shapes=[
             pltpu.VMEM((ff, cols), BF16),
             pltpu.VMEM((1, rows, cols), F32),
@@ -310,15 +322,15 @@
     ff, ranks = projector.shape
     cols = grad_slab.shape[2]
     rows = first_moment.shape[1]
-    proj, step, velocity = exchange(grad_slab, projector, first_moment, second_moment, momentum)
+    proj, step, velocity, acc = exchange(grad_slab, projector, first_moment, second_moment, momentum)
     vmem_spec = pl.BlockSpec(memory_space=pltpu.VMEM)
     any_spec = pl.BlockSpec(memory_space=pl.ANY)
-    operands = (proj, step.reshape(ranks, cols), velocity.reshape(rows, cols))
+    operands = (proj, step.reshape(ranks, cols), velocity.reshape(rows, cols), acc)
     return pl.pallas_call(
         update_kernel,
         name="update",
         out_shape=(jax.ShapeDtypeStruct((ff, cols), BF16), jax.ShapeDtypeStruct((rows, cols), F32)),
-        in_specs=[vmem_spec] * 3,
+        in_specs=[vmem_spec] * 4,
         out_specs=(any_spec, any_spec),
         scratch_shapes=[pltpu.VMEM((ff, cols), BF16), pltpu.SemaphoreType.DMA((ff // UPDATE_ROWS + 1,))],
         compiler_params=pltpu.CompilerParams(vmem_limit_bytes=16 << 20),

time: 43.8 us -> 43.3 us (0.989)
  Pallas kernels: 43 us -> 42.5 us
    pallas_call x1, Pallas kernels: 1.86 us -> 1.4 us  [local(): pl.pallas_call(update_kernel, name='update', out_shape=(jax.ShapeDtypeStr...]
where the time goes in v5:
time: 43.3 us; the launch traced here: 43.1 us
  Pallas kernels  42.5 us (98%)
  between operations  0.64 us (1%)
    pallas_call x1, Pallas kernels, exchange(): pl.pallas_call(exchange_kernel, name='exchange', out_shape=(pltpu.VMEM(pr...  41.1 us
    pallas_call x1, Pallas kernels, local(): pl.pallas_call(update_kernel, name='update', out_shape=(jax.ShapeDtypeStr...  1.4 us

profile of v5, /device:TPU:1, one launch (start us, length us, event | category | flops | bytes accessed | tf_op | source)
XLA Modules:
  0.0 43.1 jit_solution(1022774463790515360)
XLA Ops:
  0.6 41.1 %exchange.1 = (bf16[1792,512]{1,0:T(8,128)(2,1)S(1)}, bf16[4,4,4,8,384]{4,3,2,1,0:T(8,128)(2,1)S(1)}, f32[4,8,384]{2,1,0:T(8,128)S(1)}, f32[1792,384]{1,0:T(8,128)S(1)}) custom-call(bf16[1,1792,384]{2,1,0:T(8,128)(2,1)} %grad.1, bf16[1792,512]{1,0:T(8,128)(2,1)} %proj.1, f32[1,32,384]{2,1,0:T(8,128)} %first_in.1, f32[1,32,384]{2,1,0:T(8,128)} %second_in.1, ...), custom_call_target="tpu_custom_call" | custom-call | tf_op jit(solution)/shard_map/exchange/pallas_call | solution.py:280
  41.7 1.4 %update.1 = (bf16[1792,384]{1,0:T(8,128)(2,1)}, f32[32,384]{1,0:T(8,128)}) custom-call(bf16[1792,512]{1,0:T(8,128)(2,1)S(1)} %get-tuple-element.6.proj, bf16[512,384]{1,0:T(8,128)(2,1)S(1)} %bitcast.2, f32[32,384]{1,0:T(8,128)S(1)} %bitcast.3, f32[1792,384]{1,0:T(8,128)S(1)} %get-tuple-element.9.acc), custom_call_target="tpu_custom_call" | custom-call | tf_op jit(solution)/shard_map/update/pallas_call | solution.py:329
